TPU v7x, 32 devices: a whole 2x2x4 slice. The times are simulated.
32 devices in a mesh: groups: 2 (over y), row: 8 (over z, x), col: 2 (over core).
Axes of the slice: x: 2, y: 2, z: 4, core: 2. Of those that a mesh axis runs over, the one named last changes fastest.
Arguments:
- pair: bfloat16 [48, 24, 128], P(('groups', 'row'), 'col'), parts along dimension 0, may hold values from -6 to 6
- pad_mask: int32 [48], P('groups'), parts along dimension 0, may hold values 0 or 1
- token_count: int32 [2], P('groups'), parts along dimension 0, may hold values from 12 to 24
- norm_gain: float32 [2, 2, 128], replicated, may hold values from 0.1 to 1.9
- proj_in: bfloat16 [2, 128, 512], replicated, may hold values from -0.5 to 0.5
- proj_out: bfloat16 [2, 128, 128], replicated, may hold values from -0.5 to 0.5
- gate_out: bfloat16 [2, 128, 128], replicated, may hold values from -0.5 to 0.5
Outputs:
- pair_out: bfloat16 [48, 24, 128], P(('groups', 'row'), 'col'), parts along dimension 0
There are 2 independent parts, one for each index of `groups`. A program takes and returns all parts, laid end to end along the dimension named above; an argument that names none is the same for every part. Nothing has to cross between parts.
Inputs may be any that keep to these rules, and one draw needn't show every extreme that they name: `token_count`: tokens from this index on are padding.
All inputs are finite; a program needn't handle non-finite values.
Results may differ from a plain program's by a relative error of at most 0.0085.
Values may be sent and summed in bfloat16 or wider, within the bound.
A program may use at most 64 MiB of HBM per device.

v0:
```python
import jax
import jax.numpy as jnp
from jax import lax
from jax.sharding import PartitionSpec as P

EPSILON = 1e-05


def from_partner(value, axis, bit):
    mask = 2**bit
    pairs = [(source, source ^ mask) for source in range(lax.axis_size(axis))]
    return lax.ppermute(value, axis, pairs)


def layer_norm(values, gain):
    mean = jnp.mean(values, axis=-1, keepdims=True)
    centred = values - mean
    spread = jnp.mean(centred * centred, axis=-1, keepdims=True)
    return centred * lax.rsqrt(spread + EPSILON) * gain


def gated_pair(normed, weight, mask_grid):
    hidden = jnp.einsum("rnc,cd->rnd", normed, weight, preferred_element_type=jnp.float32)
    width = weight.shape[0]
    left = (
        jax.nn.sigmoid(hidden[..., 2 * width : 3 * width])
        * hidden[..., :width]
        * mask_grid[..., None]
    )
    right = (
        jax.nn.sigmoid(hidden[..., 3 * width :])
        * hidden[..., width : 2 * width]
        * mask_grid[..., None]
    )
    return (left.astype(jnp.bfloat16), right.astype(jnp.bfloat16))


def spread_out(left, right):
    moved = (
        lax.all_to_all(
            jnp.transpose(left, (2, 0, 1)), "row", split_axis=0, concat_axis=1, tiled=True
        ),
        lax.all_to_all(
            jnp.transpose(right, (2, 0, 1)), "row", split_axis=0, concat_axis=1, tiled=True
        ),
    )
    return (moved[0], moved[1])


def bring_back(product):
    moved = lax.all_to_all(product, "row", split_axis=1, concat_axis=0, tiled=True)
    return jnp.transpose(moved, (1, 2, 0))


def finish(pair, normed, product, gain_out, weight_out, weight_gate):
    gate = jax.nn.sigmoid(
        jnp.einsum("rnc,cd->rnd", normed, weight_gate, preferred_element_type=jnp.float32)
    )
    scaled = layer_norm(product.astype(jnp.float32), gain_out).astype(jnp.bfloat16)
    update = (
        jnp.einsum("rnc,cd->rnd", scaled, weight_out, preferred_element_type=jnp.float32) * gate
    )
    return (pair.astype(jnp.float32) + update).astype(jnp.bfloat16)


def outgoing(pair, row_valid, col_valid, gains, weight_in, weight_out, weight_gate):
    rows, width_cols, channels = pair.shape
    normed = layer_norm(pair.astype(jnp.float32), gains[0]).astype(jnp.bfloat16)
    picked = normed.reshape(rows, width_cols // 3, 3, channels)[:, :, 0]
    mask_grid = row_valid[:, None] * col_valid.reshape(width_cols // 3, 3)[:, 0][None, :]
    left, right = gated_pair(picked, weight_in, mask_grid)
    left, right = spread_out(left, right)
    col_index = lax.axis_index("col")
    full_left, every_right = (
        lax.all_gather(left, "col", axis=2, tiled=True),
        lax.all_gather(right, "col", axis=2, tiled=True),
    )
    full_right = lax.dynamic_slice_in_dim(every_right, col_index * width_cols, width_cols, 1)
    product = jnp.einsum("cik,cjk->cij", full_left, full_right, preferred_element_type=jnp.float32)
    product = bring_back(product.astype(jnp.bfloat16))
    return finish(pair, normed, product, gains[1], weight_out, weight_gate)


def incoming(pair, row_valid, col_valid, gains, weight_in, weight_out, weight_gate):
    rows, width_cols, channels = pair.shape
    normed = layer_norm(pair.astype(jnp.float32), gains[0]).astype(jnp.bfloat16)
    picked = normed.reshape(rows // 3, 3, width_cols, channels)[:, 0]
    mask_grid = row_valid.reshape(rows // 3, 3)[:, 0][:, None] * col_valid[None, :]
    left, right = gated_pair(picked, weight_in, mask_grid)
    left, right = spread_out(left, right)
    col_index = lax.axis_index("col")
    got = from_partner(left, "col", 0)
    full_left = jnp.where(
        col_index == 0, jnp.concatenate([left, got], axis=2), jnp.concatenate([got, left], axis=2)
    )
    product = jnp.einsum("cki,ckj->cij", full_left, right, preferred_element_type=jnp.float32)
    product = bring_back(product.astype(jnp.bfloat16))
    return finish(pair, normed, product, gains[1], weight_out, weight_gate)


def shards(pair, pad_mask, token_count, norm_gain, proj_in, proj_out, gate_out):
    rows, width_cols, channels = pair.shape
    total = pad_mask.shape[0]
    positions = jnp.arange(total, dtype=jnp.int32)
    valid = jnp.where((pad_mask > 0) & (positions < token_count[0]), 1.0, 0.0).astype(jnp.float32)
    row_valid = lax.dynamic_slice_in_dim(valid, lax.axis_index("row") * rows, rows)
    col_valid = lax.dynamic_slice_in_dim(valid, lax.axis_index("col") * width_cols, width_cols)
    first = outgoing(pair, row_valid, col_valid, norm_gain[0], proj_in[0], proj_out[0], gate_out[0])
    return incoming(first, row_valid, col_valid, norm_gain[1], proj_in[1], proj_out[1], gate_out[1])


def solution(mesh):
    in_specs = (P(("groups", "row"), "col", None), P("groups"), P("groups"), P(), P(), P(), P())
    out_specs = P(("groups", "row"), "col", None)
    return jax.shard_map(shards, mesh=mesh, in_specs=in_specs, out_specs=out_specs, check_vma=False)
```

profile of v0, /device:TPU:0, one launch (start us, length us, event | category | flops | bytes accessed | tf_op | source)
XLA Modules:
  0.0 76.6 jit_solution(682232799195613665)
XLA Ops:
  1.2 0.2 copy-done.1
  1.6 0.7 copy-done.2
  2.5 1.0 %fusion.14 = f32[3,4,512]{2,1,0:T(4,128)S(1)} fusion(bf16[2,128,512]{2,1,0:T(8,128)(2,1)} %param.11, bf16[3,4,1,128]{3,0,2,1:T(4,128)(2,1)S(1)} %slice.98), kind=kOutput, calls=%fused_computation.19 | convolution fusion | flops 1572864 | bytes 158720 | tf_op jit(solution)/shard_map/rnc,cd->rnd/dot_general | solution.py:23
  3.6 0.8 %copy.79 = bf16[128,3,4]{2,1,0:T(4,128)(2,1)} copy(bf16[128,3,4]{0,2,1:T(4,128)(2,1)S(1)} %get-tuple-element.9) | data formatting | bytes 6144 | tf_op jit(solution)/shard_map/transpose | solution.py:41
  4.5 7.3 %all-to-all-start = ((bf16[128,3,4]{2,1,0:T(4,128)(2,1)}), bf16[128,3,4]{2,1,0:T(4,128)(2,1)S(1)}, u32[]{:S(2)}, u32[]{:S(2)}) async-start(bf16[128,3,4]{2,1,0:T(4,128)(2,1)} %copy.79), calls=%async_computation | async-start | bytes 262144 | tf_op jit(solution)/shard_map/all_to_all | solution.py:40
  11.7 0.8 %copy.82 = bf16[128,3,4]{2,1,0:T(4,128)(2,1)} copy(bf16[128,3,4]{0,2,1:T(4,128)(2,1)S(1)} %get-tuple-element.10) | data formatting | bytes 6144 | tf_op jit(solution)/shard_map/transpose | solution.py:44
  12.5 6.5 %all-to-all-done = bf16[128,3,4]{2,1,0:T(4,128)(2,1)S(1)} async-done(((bf16[128,3,4]{2,1,0:T(4,128)(2,1)}), bf16[128,3,4]{2,1,0:T(4,128)(2,1)S(1)}, u32[]{:S(2)}, u32[]{:S(2)}) %all-to-all-start) | async-done | bytes 3104 | tf_op jit(solution)/shard_map/all_to_all | solution.py:40
  19.0 3.4 %all-to-all-start.1 = ((bf16[128,3,4]{2,1,0:T(4,128)(2,1)}), bf16[128,3,4]{2,1,0:T(4,128)(2,1)S(1)}, u32[]{:S(2)}, u32[]{:S(2)}) async-start(bf16[128,3,4]{2,1,0:T(4,128)(2,1)} %copy.82), calls=%async_computation.1 | async-start | bytes 262144 | tf_op jit(solution)/shard_map/all_to_all | solution.py:43
  22.4 0.2 copy.80
  22.8 1.8 %all_gather.6 = bf16[16,24,8]{1,0,2:T(8,128)(2,1)S(1)} all-gather(bf16[16,24,4]{1,0,2:T(8,128)(2,1)S(1)} %copy.81), channel_id=1, replica_groups=mesh['groups'=2,'row'=8,'col'=2] {'col'}, dimensions={2}, use_global_device_ids=true | all-gather | bytes 9216 | tf_op jit(solution)/shard_map/all_gather | solution.py:75
  24.6 5.1 %all-to-all-done.1 = bf16[128,3,4]{2,1,0:T(4,128)(2,1)S(1)} async-done(((bf16[128,3,4]{2,1,0:T(4,128)(2,1)}), bf16[128,3,4]{2,1,0:T(4,128)(2,1)S(1)}, u32[]{:S(2)}, u32[]{:S(2)}) %all-to-all-start.1) | async-done | bytes 3104 | tf_op jit(solution)/shard_map/all_to_all | solution.py:43
  29.7 0.2 copy.83
  30.0 1.8 %all_gather.7 = bf16[16,24,8]{1,0,2:T(8,128)(2,1)S(1)} all-gather(bf16[16,24,4]{1,0,2:T(8,128)(2,1)S(1)} %copy.84), channel_id=1, replica_groups=mesh['groups'=2,'row'=8,'col'=2] {'col'}, dimensions={2}, use_global_device_ids=true | all-gather | bytes 9216 | tf_op jit(solution)/shard_map/all_gather | solution.py:76
  31.9 0.2 convolution_convert_fusion.1
  32.2 0.2 copy.87
  32.5 8.9 %all_to_all.90 = bf16[8,2,288]{2,1,0:T(2,128)(2,1)S(1)} all-to-all(bf16[8,2,288]{2,1,0:T(2,128)(2,1)S(1)} %reshape.133), channel_id=1, replica_groups=mesh['groups'=2,'row'=8,'col'=2] {'row'}, dimensions={0} | all-to-all | bytes 18432 | tf_op jit(solution)/shard_map/all_to_all | solution.py:51
  41.6 0.2 copy.88
  42.4 0.4 copy-done.3
  42.8 0.2 fusion.25
  43.0 0.3 fusion.66
  43.8 0.8 %copy.91 = bf16[128,1,12]{2,1,0:T(2,128)(2,1)} copy(bf16[128,1,12]{0,2,1:T(8,128)(2,1)S(1)} %get-tuple-element.8) | data formatting | bytes 6144 | tf_op jit(solution)/shard_map/transpose | solution.py:41
  44.6 3.3 %all-to-all-start.3 = ((bf16[128,1,12]{2,1,0:T(2,128)(2,1)}), bf16[128,1,12]{2,1,0:T(2,128)(2,1)S(1)}, u32[]{:S(2)}, u32[]{:S(2)}) async-start(bf16[128,1,12]{2,1,0:T(2,128)(2,1)} %copy.91), calls=%async_computation.3 | async-start | bytes 131072 | tf_op jit(solution)/shard_map/all_to_all | solution.py:40
  47.9 0.8 copy.93
  48.7 6.1 %all-to-all-done.3 = bf16[128,1,12]{2,1,0:T(2,128)(2,1)S(1)} async-done(((bf16[128,1,12]{2,1,0:T(2,128)(2,1)}), bf16[128,1,12]{2,1,0:T(2,128)(2,1)S(1)}, u32[]{:S(2)}, u32[]{:S(2)}) %all-to-all-start.3) | async-done | bytes 3104 | tf_op jit(solution)/shard_map/all_to_all | solution.py:40
  54.8 3.3 %all-to-all-start.4 = ((bf16[128,1,12]{2,1,0:T(2,128)(2,1)}), bf16[128,1,12]{2,1,0:T(2,128)(2,1)S(1)}, u32[]{:S(2)}, u32[]{:S(2)}) async-start(bf16[128,1,12]{2,1,0:T(2,128)(2,1)} %copy.93), calls=%async_computation.4 | async-start | bytes 131072 | tf_op jit(solution)/shard_map/all_to_all | solution.py:43
  58.4 6.6 %all-to-all-done.4 = bf16[128,1,12]{2,1,0:T(2,128)(2,1)S(1)} async-done(((bf16[128,1,12]{2,1,0:T(2,128)(2,1)}), bf16[128,1,12]{2,1,0:T(2,128)(2,1)S(1)}, u32[]{:S(2)}, u32[]{:S(2)}) %all-to-all-start.4) | async-done | bytes 3104 | tf_op jit(solution)/shard_map/all_to_all | solution.py:43
  65.1 0.2 convolution_convert_fusion
  65.3 0.2 copy.97
  65.7 8.9 %all_to_all.91 = bf16[8,2,288]{2,1,0:T(2,128)(2,1)S(1)} all-to-all(bf16[8,2,288]{2,1,0:T(2,128)(2,1)S(1)} %reshape.135), channel_id=1, replica_groups=mesh['groups'=2,'row'=8,'col'=2] {'row'}, dimensions={0} | all-to-all | bytes 18432 | tf_op jit(solution)/shard_map/all_to_all | solution.py:51
  74.8 0.2 copy.98
  75.5 0.2 fusion.21
  75.7 0.8 %fusion.12 = bf16[3,12,128]{2,1,0:T(8,128)(2,1)} fusion(f32[3,12,128]{2,1,0:T(8,128)S(1)} %get-tuple-element.16, f32[3,12,128]{2,1,0:T(8,128)S(1)} %fusion.21, bf16[2,128,128]{2,1,0:T(8,128)(2,1)S(1)} %copy-done.4, f32[128]{0:T(128)S(1)} %get-tuple-element.14, f32[3,12]{1,0:T(4,128)S(1)} %add_rsqrt_fusion.1, f32[3,12]{1,0:T(4,128)S(1)} %broadcast_multiply_fusion.2), kind=kOutput, calls=%fused_computation.17 | convolution fusion | flops 1225728 | bytes 120320 | tf_op jit(solution)/shard_map/rnc,cd->rnd/dot_general | solution.py:57
  (61 shorter events, 3.8 us)
Async XLA Ops:
  0.0 0.7 copy-start.5
  0.7 0.7 copy-start.1
  1.6 0.7 copy-start.2
  4.5 14.6 %all-to-all-start = ((bf16[128,3,4]{2,1,0:T(4,128)(2,1)}), bf16[128,3,4]{2,1,0:T(4,128)(2,1)S(1)}, u32[]{:S(2)}, u32[]{:S(2)}) async-start(bf16[128,3,4]{2,1,0:T(4,128)(2,1)} %copy.79), calls=%async_computation | async-start | bytes 262144 | tf_op jit(solution)/shard_map/all_to_all | solution.py:40
  19.0 10.7 %all-to-all-start.1 = ((bf16[128,3,4]{2,1,0:T(4,128)(2,1)}), bf16[128,3,4]{2,1,0:T(4,128)(2,1)S(1)}, u32[]{:S(2)}, u32[]{:S(2)}) async-start(bf16[128,3,4]{2,1,0:T(4,128)(2,1)} %copy.82), calls=%async_computation.1 | async-start | bytes 262144 | tf_op jit(solution)/shard_map/all_to_all | solution.py:43
  42.0 0.8 %copy-start.3 = (bf16[2,128,128]{2,1,0:T(8,128)(2,1)S(1)}, bf16[2,128,128]{2,1,0:T(8,128)(2,1)}, u32[]{:S(2)}) copy-start(bf16[2,128,128]{2,1,0:T(8,128)(2,1)} %param.12) | copy-start | bytes 196612
  42.0 1.0 %copy-start.4 = (bf16[2,128,128]{2,1,0:T(8,128)(2,1)S(1)}, bf16[2,128,128]{2,1,0:T(8,128)(2,1)}, u32[]{:S(2)}) copy-start(bf16[2,128,128]{2,1,0:T(8,128)(2,1)} %param.13) | copy-start | bytes 196612
  42.1 1.5 %copy-start = (bf16[2,128,512]{2,1,0:T(8,128)(2,1)S(1)}, bf16[2,128,512]{2,1,0:T(8,128)(2,1)}, u32[]{:S(2)}) copy-start(bf16[2,128,512]{2,1,0:T(8,128)(2,1)} %param.11) | copy-start | bytes 786436
  44.6 10.2 %all-to-all-start.3 = ((bf16[128,1,12]{2,1,0:T(2,128)(2,1)}), bf16[128,1,12]{2,1,0:T(2,128)(2,1)S(1)}, u32[]{:S(2)}, u32[]{:S(2)}) async-start(bf16[128,1,12]{2,1,0:T(2,128)(2,1)} %copy.91), calls=%async_computation.3 | async-start | bytes 131072 | tf_op jit(solution)/shard_map/all_to_all | solution.py:40
  54.8 10.2 %all-to-all-start.4 = ((bf16[128,1,12]{2,1,0:T(2,128)(2,1)}), bf16[128,1,12]{2,1,0:T(2,128)(2,1)S(1)}, u32[]{:S(2)}, u32[]{:S(2)}) async-start(bf16[128,1,12]{2,1,0:T(2,128)(2,1)} %copy.93), calls=%async_computation.4 | async-start | bytes 131072 | tf_op jit(solution)/shard_map/all_to_all | solution.py:43
  58.3 6.7 %collective-permute-start = (bf16[16,8,12]{0,1,2:T(8,128)(2,1)S(1)}, bf16[16,8,12]{0,1,2:T(8,128)(2,1)S(1)}, u32[]{:S(2)}, u32[]{:S(2)}) collective-permute-start(bf16[16,8,12]{0,1,2:T(8,128)(2,1)S(1)} %bitcast.123), channel_id=1, source_target_pairs={{0,1},{1,0},{2,3},{3,2},{4,5},{5,4},{6,7},{7,6},{8,9},{9,8},{10,11... | collective-permute-start | bytes 9224 | tf_op jit(solution)/shard_map/ppermute | solution.py:12
where the time goes:
time: 77.3 us; the launch traced here: 76.6 us
  waiting for transfers between devices  24.3 us (31%)
  blocking collectives  21.5 us (28%)
  starting transfers between devices  17.4 us (23%)
  local copies, waits for them, and re-layouts  7.88 us (10%)
  matrix products  3.1 us (4%)
  other arithmetic  1.45 us (2%)
  between operations  0.94 us (1%)
    all_to_all x2, blocking collectives, bring_back(): lax.all_to_all(product, 'row', split_axis=1, concat_axis=0, tiled=True)  17.8 us
    all_to_all x2, waiting for transfers between devices, spread_out(): lax.all_to_all(jnp.transpose(left, (2, 0, 1)), 'row', split_axis=0, conca...  12.6 us
    all_to_all x2, waiting for transfers between devices, spread_out(): lax.all_to_all(jnp.transpose(right, (2, 0, 1)), 'row', split_axis=0, conc...  11.7 us
    all_to_all x2, starting transfers between devices, spread_out(): lax.all_to_all(jnp.transpose(left, (2, 0, 1)), 'row', split_axis=0, conca...  10.6 us
    all_to_all x2, starting transfers between devices, spread_out(): lax.all_to_all(jnp.transpose(right, (2, 0, 1)), 'row', split_axis=0, conc...  6.72 us
    unnamed x17, local copies, waits for them, and re-layouts  1.93 us
    all_gather x1, blocking collectives, outgoing(): lax.all_gather(left, 'col', axis=2, tiled=True)  1.83 us
    all_gather x1, blocking collectives, outgoing(): lax.all_gather(right, 'col', axis=2, tiled=True)  1.83 us
  transfers between devices with their start and end apart: 5, of which 4 were waited for; matrix products, arithmetic and copies ran while one was open for 3% of the time, Pallas kernels for 0%

commit v1 on v0

--- a/solution.py
+++ b/solution.py
@@ -1,9 +1,16 @@
+import functools
+
 import jax
 import jax.numpy as jnp
 from jax import lax
+from jax.experimental import pallas as pl
+from jax.experimental.pallas import tpu as pltpu
 from jax.sharding import PartitionSpec as P
 
 EPSILON = 1e-05
+STEP = 3
+TILE = 16
+MESH = pl.DeviceIdType.MESH
 
 
 def from_partner(value, axis, bit):
@@ -109,7 +116,327 @@
     return incoming(first, row_valid, col_valid, norm_gain[1], proj_in[1], proj_out[1], gate_out[1])
 
 
+def sigmoid(values):
+    return 0.5 * jnp.tanh(0.5 * values) + 0.5
+
+
+def narrow(values):
+    return values.astype(jnp.bfloat16)
+
+
+def rounded(values):
+    return values.astype(jnp.bfloat16).astype(jnp.float32)
+
+
+def dot(left, right):
+    return jnp.dot(left, right, preferred_element_type=jnp.float32)
+
+
+def iota(shape, axis):
+    return lax.broadcasted_iota(jnp.int32, shape, axis)
+
+
+def one_hot(index, width):
+    return narrow(jnp.where(iota((index.shape[0], width), 1) == index, 1.0, 0.0))
+
+
+def fused_kernel(
+    rows_axis,
+    width,
+    pair_hbm,
+    mask_hbm,
+    count_hbm,
+    gain_hbm,
+    in_hbm,
+    out_hbm,
+    gate_hbm,
+    result_ref,
+    pair_v,
+    mask_v,
+    count_v,
+    gain_v,
+    in_v,
+    out_v,
+    gate_v,
+    row_blocks,
+    col_blocks,
+    left_v,
+    load_sem,
+    send_row,
+    recv_row,
+    send_col,
+    recv_col,
+):
+    channels = pair_v.shape[-1]
+    total = STEP * rows_axis
+    picks = width // STEP
+    devices = 2 * rows_axis
+    row = lax.axis_index("row")
+    col = lax.axis_index("col")
+    me = row * 2 + col
+    half = row // picks
+    own_slot = 2 * picks
+
+    loads = [
+        pltpu.make_async_copy(source, target, load_sem.at[at])
+        for at, (source, target) in enumerate(
+            [
+                (pair_hbm, pair_v),
+                (mask_hbm, mask_v),
+                (count_hbm, count_v),
+                (gain_hbm, gain_v),
+                (in_hbm, in_v),
+                (out_hbm, out_v),
+                (gate_hbm, gate_v),
+            ]
+        )
+    ]
+    loads[0].start()
+
+    col_blocks[...] = jnp.zeros_like(col_blocks)
+    peers = []
+    for offset in range(1, devices):
+        peer = lax.rem(me + offset, devices)
+        peers.append((peer, {"row": peer // 2, "col": lax.rem(peer, 2)}))
+    barrier = pltpu.get_barrier_semaphore()
+    for _, where in peers:
+        pl.semaphore_signal(barrier, inc=1, device_id=where, device_id_type=MESH)
+    for load in loads[1:]:
+        load.start()
+
+    loads[0].wait()
+    pad = jnp.zeros((TILE - width, channels), jnp.float32)
+    own = jnp.concatenate(
+        [piece for t in range(STEP) for piece in (pair_v[t].astype(jnp.float32), pad)], axis=0
+    )
+    row_blocks[me] = narrow(own[:TILE])
+    spot = iota((TILE, 1), 0)
+    spot = jnp.where(spot < STEP * picks, spot // picks * TILE + spot % picks * STEP, -1)
+    picked = narrow(dot(one_hot(spot, STEP * TILE), narrow(own)))
+    col_blocks[own_slot + col] = picked
+
+    @pl.when(col == half)
+    def _():
+        col_blocks[lax.rem(row, picks) * 2 + col] = picked
+
+    pl.semaphore_wait(barrier, devices - 1)
+
+    def row_copy(block, slot, where):
+        return pltpu.make_async_remote_copy(
+            src_ref=row_blocks.at[me],
+            dst_ref=row_blocks.at[block],
+            send_sem=send_row.at[slot],
+            recv_sem=recv_row.at[block],
+            device_id=where,
+            device_id_type=MESH,
+        )
+
+    def col_copy(block, slot, where):
+        return pltpu.make_async_remote_copy(
+            src_ref=col_blocks.at[own_slot + col],
+            dst_ref=col_blocks.at[block],
+            send_sem=send_col.at[slot],
+            recv_sem=recv_col.at[block],
+            device_id=where,
+            device_id_type=MESH,
+        )
+
+    sends = []
+    my_slot = lax.rem(row, picks) * 2 + col
+    sibling = {"row": row, "col": 1 - col}
+    for at in range(devices - 1):
+        copy = row_copy(me, at, peers[at][1])
+        copy.start()
+        sends.append(copy)
+    for step in range(1, rows_axis):
+        copy = col_copy(my_slot, step, {"row": lax.rem(row + step, rows_axis), "col": half})
+        copy.start()
+        sends.append(copy)
+    copy = col_copy(own_slot + col, rows_axis, sibling)
+    copy.start()
+    sends.append(copy)
+    extra = col_copy(my_slot, 0, sibling)
+
+    @pl.when(col != half)
+    def _():
+        extra.start()
+
+    def token_index(spot):
+        inner = jnp.where(spot < width, col * width + spot, row * STEP + spot - width)
+        return jnp.where(spot < width + STEP, inner, -1)
+
+    summed = rows_axis
+    n_left = summed * summed
+    place = iota((n_left, 1), 0)
+    a, k = place // summed, place % summed
+    left_from = (a * 2 + k // picks) * TILE + k % picks * STEP
+    place = iota((summed * TILE, 1), 0)
+    a, j = place // TILE, place % TILE
+    inside = jnp.where(
+        j < width, (a * 2 + col) * TILE + j, (a * 2 + half) * TILE + STEP * (row % picks) + j - width
+    )
+    cross_from = jnp.where(j < width + STEP, inside, -1)
+    select_rows = jnp.concatenate(
+        [one_hot(left_from, devices * TILE), one_hot(cross_from, devices * TILE)], axis=0
+    )
+    slots = (own_slot + 2) * TILE
+    place = iota((STEP * summed, 1), 0)
+    t, k = place // summed, place % summed
+    mine_from = (own_slot + k // picks) * TILE + t * picks + k % picks
+    place = iota((summed * TILE, 1), 0)
+    k, j = place // TILE, place % TILE
+    inside = jnp.where(
+        j < width,
+        (j // STEP * 2 + k // picks) * TILE + j % STEP * picks + k % picks,
+        (own_slot + k // picks) * TILE + (j - width) * picks + k % picks,
+    )
+    right_from = jnp.where(j < width + STEP, inside, -1)
+    select_cols = jnp.concatenate([one_hot(mine_from, slots), one_hot(right_from, slots)], axis=0)
+
+    for load in loads[1:4]:
+        load.wait()
+    lanes = iota((1, total), 1)
+    valid = jnp.where((mask_v[...] > 0) & (lanes < count_v[...]), 1.0, 0.0)
+
+    def pair_mask(first_index, second_index):
+        grid = iota((first_index.shape[0], total), 1)
+        both = jnp.where(grid == first_index, valid, 0.0) + jnp.where(
+            grid == second_index, valid, 0.0
+        )
+        return jnp.where(jnp.sum(both, axis=-1, keepdims=True) > 1.5, 1.0, 0.0)
+
+    place = iota(((summed + STEP) * summed, 1), 0)
+    a, k = place // summed, place % summed
+    left_mask = pair_mask(jnp.where(a < summed, STEP * a, row * STEP + a - summed), STEP * k)
+    place = iota((summed * TILE, 1), 0)
+    right_mask = pair_mask(token_index(place % TILE), STEP * (place // TILE))
+
+    for load in loads[4:]:
+        load.wait()
+
+    for peer, where in peers:
+        row_copy(peer, 0, where).wait_recv()
+    for slot in range(own_slot):
+        source = col * picks * 2 + slot
+
+        @pl.when(source != me)
+        def _():
+            col_copy(slot, 0, sibling).wait_recv()
+
+    col_copy(own_slot + 1 - col, 0, sibling).wait_recv()
+
+    from_rows = dot(select_rows, row_blocks[...].reshape(devices * TILE, channels))
+    from_cols = dot(select_cols, col_blocks[...].reshape(slots, channels))
+    n_cross = summed * TILE
+    block = jnp.concatenate([from_rows[n_left:], own], axis=0)
+    normed = narrow(layer_norm(block, gain_v[0, 0][None]))
+    side = jnp.concatenate([from_rows[:n_left], from_cols], axis=0)
+    side = narrow(layer_norm(side, gain_v[0, 0][None]))
+    n_side = n_left + STEP * summed
+    gate = sigmoid(dot(normed, gate_v[0]))
+
+    def gated(values, which, form, mask):
+        value = dot(values, in_v[form, :, which * channels : (which + 1) * channels])
+        opened = dot(values, in_v[form, :, (which + 2) * channels : (which + 3) * channels])
+        return rounded(sigmoid(opened) * value * mask)
+
+    left_v[0:n_side] = gated(side[:n_side], 0, 0, left_mask)
+    right = gated(side[n_side:], 1, 0, right_mask)
+
+    def finished(block, product, gate, form):
+        scaled = narrow(layer_norm(rounded(product), gain_v[form, 1][None]))
+        return rounded(block + dot(scaled, out_v[form]) * gate)
+
+    def multiplied(row_of, count):
+        products = []
+        for a in range(count):
+            acc = None
+            for k in range(summed):
+                at = row_of(a, k)
+                term = left_v[at : at + 1] * right[k * TILE : (k + 1) * TILE]
+                acc = term if acc is None else acc + term
+            products.append(acc)
+        return jnp.concatenate(products, axis=0)
+
+    first = finished(block, multiplied(lambda a, k: a * summed + k, summed + STEP), gate, 0)
+
+    normed = narrow(layer_norm(first, gain_v[1, 0][None]))
+    gate = sigmoid(dot(normed[n_cross:], gate_v[1]))
+    left_v[0:n_cross] = gated(normed[:n_cross], 0, 1, right_mask)
+    right = gated(normed[:n_cross], 1, 1, right_mask)
+    product = multiplied(lambda a, k: k * TILE + width + a, STEP)
+    result = narrow(finished(first[n_cross:], product, gate, 1))
+    for t in range(STEP):
+        result_ref[t] = result[t * TILE : t * TILE + width]
+
+    for copy in sends:
+        copy.wait_send()
+
+    @pl.when(col != half)
+    def _():
+        extra.wait_send()
+
+
+def fused(pair, pad_mask, token_count, norm_gain, proj_in, proj_out, gate_out):
+    rows, width, channels = pair.shape
+    rows_axis = lax.axis_size("row")
+    devices = 2 * rows_axis
+    picks = width // STEP
+    slots = 2 * picks + 2
+    args = (
+        pair,
+        pad_mask.reshape(1, -1),
+        token_count.reshape(1, 1),
+        norm_gain,
+        proj_in,
+        proj_out,
+        gate_out,
+    )
+    return pl.pallas_call(
+        functools.partial(fused_kernel, rows_axis, width),
+        out_shape=jax.ShapeDtypeStruct(pair.shape, pair.dtype),
+        in_specs=[pl.BlockSpec(memory_space=pl.ANY)] * len(args),
+        out_specs=pl.BlockSpec(memory_space=pltpu.VMEM),
+        scratch_shapes=[pltpu.VMEM(arg.shape, arg.dtype) for arg in args]
+        + [
+            pltpu.VMEM((devices, TILE, channels), jnp.bfloat16),
+            pltpu.VMEM((slots, TILE, channels), jnp.bfloat16),
+            pltpu.VMEM((rows_axis * TILE, channels), jnp.float32),
+            pltpu.SemaphoreType.DMA((len(args),)),
+            pltpu.SemaphoreType.DMA((devices - 1,)),
+            pltpu.SemaphoreType.DMA((devices,)),
+            pltpu.SemaphoreType.DMA((rows_axis + 1,)),
+            pltpu.SemaphoreType.DMA((slots,)),
+        ],
+        compiler_params=pltpu.CompilerParams(
+            collective_id=0, has_side_effects=True, vmem_limit_bytes=32 * 1024 * 1024
+        ),
+        name="fused",
+    )(*args)
+
+
+def pick(mesh):
+    def apply(pair, *rest):
+        rows, width, _ = pair.shape
+        rows_axis = mesh.shape["row"]
+        small = (
+            rows == STEP
+            and mesh.shape["col"] == 2
+            and 2 * width == STEP * rows_axis
+            and width % STEP == 0
+            and width + STEP <= TILE
+        )
+        return (fused if small else shards)(pair, *rest)
+
+    return apply
+
+
 def solution(mesh):
     in_specs = (P(("groups", "row"), "col", None), P("groups"), P("groups"), P(), P(), P(), P())
     out_specs = P(("groups", "row"), "col", None)
-    return jax.shard_map(shards, mesh=mesh, in_specs=in_specs, out_specs=out_specs, check_vma=False)
+    return jax.shard_map(
+        pick(mesh), mesh=mesh,
+        in_specs=in_specs,
+        out_specs=out_specs,
+        check_vma=False,
+    )

time: 77.3 us -> 16.9 us (0.22)
  the two profiles are of different devices: /device:TPU:0 before, /device:TPU:1 now
where the time goes in v1:
time: 16.9 us; the launch traced here: 16.6 us
  Pallas kernels  11.3 us (67%)
  local copies, waits for them, and re-layouts  4.61 us (27%)
  between operations  0.68 us (4%)
    pallas_call x1, Pallas kernels, fused(): pl.pallas_call(functools.partial(fused_kernel, rows_axis, width), out_sha...  11.3 us
    unnamed x13, local copies, waits for them, and re-layouts  4.61 us

profile of v1, /device:TPU:1, one launch (start us, length us, event | category | flops | bytes accessed | tf_op | source)
XLA Modules:
  0.0 16.6 jit_solution(2538340065776427889)
XLA Ops:
  0.7 0.0 copy-start.4
  0.7 0.0 copy-start.5
  0.7 0.7 %copy-done.4 = f32[2,2,128]{2,1,0:T(2,128)S(1)} copy-done((f32[2,2,128]{2,1,0:T(2,128)S(1)}, f32[2,2,128]{2,1,0:T(2,128)}, u32[]{:S(2)}) %copy-start.4) | copy-done | bytes 2072
  1.3 0.0 copy-done.5
  1.3 0.0 copy-start
  1.3 0.9 %copy-done = bf16[2,128,512]{2,1,0:T(8,128)(2,1)S(1)} copy-done((bf16[2,128,512]{2,1,0:T(8,128)(2,1)S(1)}, bf16[2,128,512]{2,1,0:T(8,128)(2,1)}, u32[]{:S(2)}) %copy-start) | copy-done | bytes 262168
  2.3 0.0 copy-start.1
  2.3 0.8 %copy-done.1 = bf16[2,128,128]{2,1,0:T(8,128)(2,1)S(1)} copy-done((bf16[2,128,128]{2,1,0:T(8,128)(2,1)S(1)}, bf16[2,128,128]{2,1,0:T(8,128)(2,1)}, u32[]{:S(2)}) %copy-start.1) | copy-done | bytes 65560
  3.1 0.0 copy-start.2
  3.1 0.8 %copy-done.2 = bf16[2,128,128]{2,1,0:T(8,128)(2,1)S(1)} copy-done((bf16[2,128,128]{2,1,0:T(8,128)(2,1)S(1)}, bf16[2,128,128]{2,1,0:T(8,128)(2,1)}, u32[]{:S(2)}) %copy-start.2) | copy-done | bytes 65560
  4.0 0.0 copy-start.3
  4.0 0.7 %copy-done.3 = bf16[3,12,128]{2,1,0:T(8,128)(2,1)S(1)} copy-done((bf16[3,12,128]{2,1,0:T(8,128)(2,1)S(1)}, bf16[3,12,128]{2,1,0:T(8,128)(2,1)}, u32[]{:S(2)}) %copy-start.3) | copy-done | bytes 9240
  4.7 11.3 %fused.1 = bf16[3,12,128]{2,1,0:T(8,128)(2,1)S(1)} custom-call(bf16[3,12,128]{2,1,0:T(8,128)(2,1)S(1)} %copy-done.3, s32[1,24]{1,0:T(1,128)S(1)} %bitcast.3, s32[1,1]{1,0:T(1,128)} %bitcast.2.count_hbm, f32[2,2,128]{2,1,0:T(2,128)S(1)} %copy-done.4, bf16[2,128,512]{2,1,0:T(8,128)(2,1)S(1)} %copy-done, bf16[2,128,128]{2,1,0:T(8,128)(2,1)S(1)} %copy-done.1, ...), custom_call_target="tpu_custom_call" | custom-call | tf_op jit(solution)/shard_map/fused/pallas_call | solution.py:395
  16.0 0.6 %copy.10 = bf16[3,12,128]{2,1,0:T(8,128)(2,1)} copy(bf16[3,12,128]{2,1,0:T(8,128)(2,1)S(1)} %fused.1) | data formatting | bytes 18432
Async XLA Ops:
  0.7 0.7 %copy-start.4 = (f32[2,2,128]{2,1,0:T(2,128)S(1)}, f32[2,2,128]{2,1,0:T(2,128)}, u32[]{:S(2)}) copy-start(f32[2,2,128]{2,1,0:T(2,128)} %gain_hbm.1) | copy-start | bytes 6148
  0.7 0.7 %copy-start.5 = (s32[24]{0:T(128)S(1)}, s32[24]{0:T(128)}, u32[]{:S(2)}) copy-start(s32[24]{0:T(128)} %param.8) | copy-start | bytes 292
  1.3 1.0 %copy-start = (bf16[2,128,512]{2,1,0:T(8,128)(2,1)S(1)}, bf16[2,128,512]{2,1,0:T(8,128)(2,1)}, u32[]{:S(2)}) copy-start(bf16[2,128,512]{2,1,0:T(8,128)(2,1)} %in_hbm.1) | copy-start | bytes 786436
  2.3 0.8 %copy-start.1 = (bf16[2,128,128]{2,1,0:T(8,128)(2,1)S(1)}, bf16[2,128,128]{2,1,0:T(8,128)(2,1)}, u32[]{:S(2)}) copy-start(bf16[2,128,128]{2,1,0:T(8,128)(2,1)} %out_hbm.1) | copy-start | bytes 196612
  3.1 0.8 %copy-start.2 = (bf16[2,128,128]{2,1,0:T(8,128)(2,1)S(1)}, bf16[2,128,128]{2,1,0:T(8,128)(2,1)}, u32[]{:S(2)}) copy-start(bf16[2,128,128]{2,1,0:T(8,128)(2,1)} %gate_hbm.1) | copy-start | bytes 196612
  4.0 0.7 %copy-start.3 = (bf16[3,12,128]{2,1,0:T(8,128)(2,1)S(1)}, bf16[3,12,128]{2,1,0:T(8,128)(2,1)}, u32[]{:S(2)}) copy-start(bf16[3,12,128]{2,1,0:T(8,128)(2,1)} %pair_hbm.1) | copy-start | bytes 27652

commit v2 on v1

--- a/solution.py
+++ b/solution.py
@@ -395,7 +395,7 @@
     return pl.pallas_call(
         functools.partial(fused_kernel, rows_axis, width),
         out_shape=jax.ShapeDtypeStruct(pair.shape, pair.dtype),
-        in_specs=[pl.BlockSpec(memory_space=pl.ANY)] * len(args),
+        in_specs=[pl.BlockSpec(memory_space=pltpu.HBM)] * len(args),
         out_specs=pl.BlockSpec(memory_space=pltpu.VMEM),
         scratch_shapes=[pltpu.VMEM(arg.shape, arg.dtype) for arg in args]
         + [
@@ -435,7 +435,8 @@
     in_specs = (P(("groups", "row"), "col", None), P("groups"), P("groups"), P(), P(), P(), P())
     out_specs = P(("groups", "row"), "col", None)
     return jax.shard_map(
-        pick(mesh), mesh=mesh,
+        pick(mesh),
+        mesh=mesh,
         in_specs=in_specs,
         out_specs=out_specs,
         check_vma=False,

time: 16.9 us -> 16.9 us (level)
  no operation moved by 1% of the time
where the time goes in v2:
time: 16.9 us; the launch traced here: 16.6 us
  Pallas kernels  11.3 us (67%)
  local copies, waits for them, and re-layouts  4.61 us (27%)
  between operations  0.68 us (4%)
    pallas_call x1, Pallas kernels, fused(): pl.pallas_call(functools.partial(fused_kernel, rows_axis, width), out_sha...  11.3 us
    unnamed x13, local copies, waits for them, and re-layouts  4.61 us

profile of v2, /device:TPU:1, one launch (start us, length us, event | category | flops | bytes accessed | tf_op | source)
XLA Modules:
  0.0 16.6 jit_solution(2538340065776427889)
XLA Ops:
  0.7 0.0 copy-start.4
  0.7 0.0 copy-start.5
  0.7 0.7 %copy-done.4 = f32[2,2,128]{2,1,0:T(2,128)S(1)} copy-done((f32[2,2,128]{2,1,0:T(2,128)S(1)}, f32[2,2,128]{2,1,0:T(2,128)}, u32[]{:S(2)}) %copy-start.4) | copy-done | bytes 2072
  1.3 0.0 copy-done.5
  1.3 0.0 copy-start
  1.3 0.9 %copy-done = bf16[2,128,512]{2,1,0:T(8,128)(2,1)S(1)} copy-done((bf16[2,128,512]{2,1,0:T(8,128)(2,1)S(1)}, bf16[2,128,512]{2,1,0:T(8,128)(2,1)}, u32[]{:S(2)}) %copy-start) | copy-done | bytes 262168
  2.3 0.0 copy-start.1
  2.3 0.8 %copy-done.1 = bf16[2,128,128]{2,1,0:T(8,128)(2,1)S(1)} copy-done((bf16[2,128,128]{2,1,0:T(8,128)(2,1)S(1)}, bf16[2,128,128]{2,1,0:T(8,128)(2,1)}, u32[]{:S(2)}) %copy-start.1) | copy-done | bytes 65560
  3.1 0.0 copy-start.2
  3.1 0.8 %copy-done.2 = bf16[2,128,128]{2,1,0:T(8,128)(2,1)S(1)} copy-done((bf16[2,128,128]{2,1,0:T(8,128)(2,1)S(1)}, bf16[2,128,128]{2,1,0:T(8,128)(2,1)}, u32[]{:S(2)}) %copy-start.2) | copy-done | bytes 65560
  4.0 0.0 copy-start.3
  4.0 0.7 %copy-done.3 = bf16[3,12,128]{2,1,0:T(8,128)(2,1)S(1)} copy-done((bf16[3,12,128]{2,1,0:T(8,128)(2,1)S(1)}, bf16[3,12,128]{2,1,0:T(8,128)(2,1)}, u32[]{:S(2)}) %copy-start.3) | copy-done | bytes 9240
  4.7 11.3 %fused.1 = bf16[3,12,128]{2,1,0:T(8,128)(2,1)S(1)} custom-call(bf16[3,12,128]{2,1,0:T(8,128)(2,1)S(1)} %copy-done.3, s32[1,24]{1,0:T(1,128)S(1)} %bitcast.3, s32[1,1]{1,0:T(1,128)} %bitcast.2.count_hbm, f32[2,2,128]{2,1,0:T(2,128)S(1)} %copy-done.4, bf16[2,128,512]{2,1,0:T(8,128)(2,1)S(1)} %copy-done, bf16[2,128,128]{2,1,0:T(8,128)(2,1)S(1)} %copy-done.1, ...), custom_call_target="tpu_custom_call" | custom-call | tf_op jit(solution)/shard_map/fused/pallas_call | solution.py:395
  16.0 0.6 %copy.10 = bf16[3,12,128]{2,1,0:T(8,128)(2,1)} copy(bf16[3,12,128]{2,1,0:T(8,128)(2,1)S(1)} %fused.1) | data formatting | bytes 18432
Async XLA Ops:
  0.7 0.7 %copy-start.4 = (f32[2,2,128]{2,1,0:T(2,128)S(1)}, f32[2,2,128]{2,1,0:T(2,128)}, u32[]{:S(2)}) copy-start(f32[2,2,128]{2,1,0:T(2,128)} %gain_hbm.1) | copy-start | bytes 6148
  0.7 0.7 %copy-start.5 = (s32[24]{0:T(128)S(1)}, s32[24]{0:T(128)}, u32[]{:S(2)}) copy-start(s32[24]{0:T(128)} %param.8) | copy-start | bytes 292
  1.3 1.0 %copy-start = (bf16[2,128,512]{2,1,0:T(8,128)(2,1)S(1)}, bf16[2,128,512]{2,1,0:T(8,128)(2,1)}, u32[]{:S(2)}) copy-start(bf16[2,128,512]{2,1,0:T(8,128)(2,1)} %in_hbm.1) | copy-start | bytes 786436
  2.3 0.8 %copy-start.1 = (bf16[2,128,128]{2,1,0:T(8,128)(2,1)S(1)}, bf16[2,128,128]{2,1,0:T(8,128)(2,1)}, u32[]{:S(2)}) copy-start(bf16[2,128,128]{2,1,0:T(8,128)(2,1)} %out_hbm.1) | copy-start | bytes 196612
  3.1 0.8 %copy-start.2 = (bf16[2,128,128]{2,1,0:T(8,128)(2,1)S(1)}, bf16[2,128,128]{2,1,0:T(8,128)(2,1)}, u32[]{:S(2)}) copy-start(bf16[2,128,128]{2,1,0:T(8,128)(2,1)} %gate_hbm.1) | copy-start | bytes 196612
  4.0 0.7 %copy-start.3 = (bf16[3,12,128]{2,1,0:T(8,128)(2,1)S(1)}, bf16[3,12,128]{2,1,0:T(8,128)(2,1)}, u32[]{:S(2)}) copy-start(bf16[3,12,128]{2,1,0:T(8,128)(2,1)} %pair_hbm.1) | copy-start | bytes 27652
